TPU v7x, 32 devices: a whole 2x2x4 slice. The times are simulated.
32 devices in a mesh: rows: 16 (over z, y, core), rep: 2 (over x).
Axes of the slice: x: 2, y: 2, z: 4, core: 2. Of those that a mesh axis runs over, the one named last changes fastest.
Arguments:
- features: bfloat16 [16384, 256], P('rows'), may hold values from -6 to 6
- inv_sqrt_degree: bfloat16 [16384], P('rows'), may hold values from 0.25 to 1
- weight: bfloat16 [256, 256], replicated, may hold values from -0.375 to 0.375
- tile_vals: bfloat16 [16, 512, 128, 128], P('rows', 'rep'), may hold values from -0.0625 to 0.0625
- tile_row: int32 [16, 512], P('rows', 'rep'), may hold values from 0 to 7, as said below
- tile_col: int32 [16, 512], P('rows', 'rep'), may hold values from 0 to 63, as said below
- tile_count: int32 [16, 16], P('rows', 'rep'), may hold values from 0 to 64, as said below
- cotangent: bfloat16 [16384, 256], P('rows'), may hold values from -6 to 6
Outputs:
- activated: bfloat16 [16384, 256], P(('rows', 'rep'))
- weight_grad: float32 [256, 256], replicated
- feature_grad: bfloat16 [16384, 256], P(('rep', 'rows'))
Inputs may be any that keep to these rules, and one draw needn't show every extreme that they name: `tile_count`: each count is at most 64; the 8 counts of row block i and columns r * 8 .. r * 8 + 7 sum to at most 256. Some pair holds exactly 64 tiles and some block row and replica exactly 256, in every draw. `tile_row`: the valid slots of a block row and replica are ordered by column block, and inside one block pair their positions are distinct. A valid slot counted for column block r * 8 + s has tile_col between s * 8 and s * 8 + 7.
All inputs are finite; a program needn't handle non-finite values.
Results may differ from a plain program's by a relative error of at most 0.015.
Values may be sent and summed in bfloat16 or wider, within the bound.
A program may use at most 128 MiB of HBM per device.

v0:
```python
import jax
import jax.numpy as jnp
from jax import lax
from jax.sharding import PartitionSpec as P


def from_root(shard, axis, root):
    mine = lax.axis_index(axis) == root
    return lax.psum(jnp.where(mine, shard, jnp.zeros_like(shard)), axis)


def tile_products(values, out_index, in_index, keep, source, out_tiles, flipped):
    count = values.shape[0]
    block_size = 32
    turns = count // block_size
    width = source.shape[-1]
    tile = values.shape[-1]

    def advance(carry, block):
        vals_block, out_block, in_block, keep_block = block
        picked = source[in_block]
        if flipped:
            prod = jnp.einsum(
                "kji,kjf->kif", vals_block, picked, preferred_element_type=jnp.float32
            )
        else:
            prod = jnp.einsum(
                "kij,kjf->kif", vals_block, picked, preferred_element_type=jnp.float32
            )
        prod = jnp.where(keep_block[:, None, None], prod, jnp.float32(0.0))
        return (carry.at[out_block].add(prod), None)

    blocks = (
        values.reshape(turns, block_size, tile, tile),
        out_index.reshape(turns, block_size),
        in_index.reshape(turns, block_size),
        keep.reshape(turns, block_size),
    )
    initial = jnp.zeros((out_tiles, tile, width), jnp.float32)
    result, _ = lax.scan(advance, initial, blocks)
    return result


def section_window(values, out_rows, in_cols, starts, ends, section, per_block):
    slots = values.shape[0]
    pair_slots = per_block * per_block
    first = jnp.clip(starts[section], 0, slots - pair_slots)
    index = first + jnp.arange(pair_slots, dtype=jnp.int32)
    keep = (index >= starts[section]) & (index < ends[section])
    vals_window = lax.dynamic_slice_in_dim(values, first, pair_slots, 0)
    rows_window = lax.dynamic_slice_in_dim(out_rows, first, pair_slots, 0)
    cols_window = lax.dynamic_slice_in_dim(in_cols, first, pair_slots, 0)
    cols_window = jnp.clip(cols_window - section * per_block, 0, per_block - 1)
    return (vals_window, rows_window, cols_window, keep)


def shards(features, inv_sqrt_degree, weight, tile_vals, tile_row, tile_col, tile_count, cotangent):
    rows_count = lax.axis_size("rows")
    rep_count = lax.axis_size("rep")
    sections = rows_count // rep_count
    replica = lax.axis_index("rep")
    block_row = lax.axis_index("rows")
    nodes_block, width = features.shape
    tile = tile_vals.shape[-1]
    per_block = nodes_block // tile
    share = nodes_block // rep_count
    values = tile_vals[0]
    out_rows = tile_row[0]
    in_cols = tile_col[0]
    counts = tile_count[0]
    degree = inv_sqrt_degree.astype(jnp.float32)[:, None]
    scaled = (degree * features.astype(jnp.float32)).astype(jnp.bfloat16)
    ends = jnp.cumsum(counts)
    starts = ends - counts
    grad_factor = float(nodes_block * rows_count) ** (-0.5)
    arrived = []
    forward_sum = jnp.zeros((per_block, tile, width), jnp.float32)
    for section in range(sections):
        root = replica * sections + section
        block_feats, block_degree = (
            from_root(scaled, "rows", root),
            from_root(inv_sqrt_degree, "rows", root),
        )
        arrived.append((block_feats, block_degree))
        vals_window, rows_window, cols_window, keep = section_window(
            values, out_rows, in_cols, starts, ends, section, per_block
        )
        source = block_feats.reshape(per_block, tile, width)
        forward_sum = forward_sum + tile_products(
            vals_window, rows_window, cols_window, keep, source, per_block, False
        )
    partial_rows = forward_sum.reshape(nodes_block, width)
    summed = lax.psum(partial_rows, "rep")
    propagated = (degree * (summed + scaled.astype(jnp.float32))).astype(jnp.bfloat16)
    preact = jnp.dot(propagated, weight, preferred_element_type=jnp.float32)
    gate = jax.nn.sigmoid(preact)
    activated_block = (preact * gate).astype(jnp.bfloat16)
    grad_pre = (cotangent.astype(jnp.float32) * gate * (1.0 + preact * (1.0 - gate))).astype(
        jnp.bfloat16
    )
    back = (degree * jnp.dot(grad_pre, weight.T, preferred_element_type=jnp.float32)).astype(
        jnp.bfloat16
    )
    activated = lax.dynamic_slice_in_dim(activated_block, replica * share, share, 0)
    prop_share = lax.dynamic_slice_in_dim(propagated, replica * share, share, 0)
    grad_share = lax.dynamic_slice_in_dim(grad_pre, replica * share, share, 0)
    local_grad = lax.dot_general(
        prop_share, grad_share, (((0,), (0,)), ((), ())), preferred_element_type=jnp.float32
    )
    weight_grad = lax.psum(local_grad * grad_factor, ("rows", "rep"))
    back_tiles = back.reshape(per_block, tile, width)
    pieces = []
    for section in range(sections):
        vals_window, rows_window, cols_window, keep = section_window(
            values, out_rows, in_cols, starts, ends, section, per_block
        )
        pieces.append(
            tile_products(vals_window, cols_window, rows_window, keep, back_tiles, per_block, True)
        )
    terms = jnp.stack(pieces).reshape(sections, nodes_block, width)
    own_section = block_row - replica * sections
    section_ids = jnp.arange(sections, dtype=jnp.int32)
    self_part = jnp.where(
        (section_ids == own_section)[:, None, None],
        back.astype(jnp.float32)[None, :, :],
        jnp.float32(0.0),
    )
    degrees = jnp.stack([pair[1] for pair in arrived]).astype(jnp.float32)
    terms = (terms + self_part) * degrees[:, :, None]
    feature_grad = lax.psum_scatter(
        terms.reshape(sections * nodes_block, width), "rows", scatter_dimension=0, tiled=True
    ).astype(jnp.bfloat16)
    return (activated, weight_grad, feature_grad)


def solution(mesh):
    placed = (
        P("rows", None),
        P("rows"),
        P(),
        P("rows", "rep", None, None),
        P("rows", "rep"),
        P("rows", "rep"),
        P("rows", "rep"),
        P("rows", None),
    )
    return jax.shard_map(
        shards,
        mesh=mesh,
        in_specs=placed,
        out_specs=(P(("rows", "rep"), None), P(), P(("rep", "rows"), None)),
        check_vma=False,
    )
```

profile of v0, /device:TPU:0, one launch (start us, length us, event | category | flops | bytes accessed | tf_op | source)
XLA Modules:
  0.0 884.7 jit_solution(16465875463462751879)
XLA Ops:
  23.0 64.5 %all-reduce = (bf16[1,1024,1]{1,2,0:T(2,128)(2,1)S(1)}, bf16[1,1024,1]{1,2,0:T(2,128)(2,1)}, bf16[1,1024,1]{1,2,0:T(2,128)(2,1)}, bf16[1,1024,1]{1,2,0:T(2,128)(...) all-reduce(bf16[1,1024,1]{1,2,0:T(2,128)(2,1)S(1)} %stack.66, ...), channel_id=1, replica_groups=mesh['rows'=16,'rep'=2] {'rows'}, use_global_device_ids=true, to_apply=%region_59.60 | all-reduce | flops 8192 | bytes 32768 | tf_op jit(solution)/shard_map/psum | solution.py:9
  100.7 12.1 %constant_dynamic-slice_fusion.51 = (bf16[1,64,128,128]{3,2,1,0:T(8,128)(2,1)}, bf16[1,64,128,128]{3,2,1,0:T(8,128)(2,1)}, bf16[1,64,128,128]{3,2,1,0:T(8,128)(2...) fusion(bf16[1,256,128,128]{3,2,1,0:T(8,128)(2,1)} %param.43, ...), kind=kLoop, calls=%fused_computation.317 | loop fusion | bytes 33554464 | tf_op jit(solution)/shard_map/dynamic_slice | solution.py:50
  112.8 16.7 %all-reduce.10.cloned.1.call-done = (bf16[8,128,256]{2,1,0:T(8,128)(2,1)}, bf16[8,128,256]{2,1,0:T(8,128)(2,1)}, bf16[8,128,256]{2,1,0:T(8,128)(2,1)}, bf16[8,12...) async-done(((bf16[8,128,256]{2,1,0:T(8,128)(2,1)}, ...) | async-done | bytes 4194320 | tf_op jit(solution)/shard_map/psum | solution.py:9
  129.6 28.4 %while.167 = (s32[]{:T(128)}, f32[8,128,256]{2,1,0:T(8,128)S(1)}, s32[2,32]{1,0:T(2,128)S(1)}, pred[2,32]{1,0:T(4,128)(4,1)S(1)}, bf16[2,32,128,128]{3,2,1,0:T(8...) while((s32[]{:T(128)}, f32[8,128,256]{2,1,0:T(8,128)S(1)}, ...), condition=%wide.region_32.33_spmd, body=%wide.region_30.32_spmd.sunk | while | flops 270533824 | bytes 24122440 | solution.py:40
  137.4 6.4 scatter_fusion.7
  151.6 6.4 scatter_fusion.7
  159.0 26.3 %while.166 = (s32[]{:T(128)}, f32[8,128,256]{2,1,0:T(8,128)S(1)}, s32[2,32]{1,0:T(2,128)S(1)}, pred[2,32]{1,0:T(4,128)(4,1)S(1)}, bf16[2,32,128,128]{3,2,1,0:T(8...) while((s32[]{:T(128)}, f32[8,128,256]{2,1,0:T(8,128)S(1)}, ...), condition=%wide.region_28.29_spmd, body=%wide.region_26.28_spmd.sunk | while | flops 270533824 | bytes 24122440 | solution.py:40
  165.7 6.5 scatter_fusion.6
  178.9 6.4 scatter_fusion.6
  186.4 26.3 %while.165 = (s32[]{:T(128)}, f32[8,128,256]{2,1,0:T(8,128)S(1)}, s32[2,32]{1,0:T(2,128)S(1)}, pred[2,32]{1,0:T(4,128)(4,1)S(1)}, bf16[2,32,128,128]{3,2,1,0:T(8...) while((s32[]{:T(128)}, f32[8,128,256]{2,1,0:T(8,128)S(1)}, ...), condition=%wide.region_24.25_spmd, body=%wide.region_22.24_spmd.sunk | while | flops 270533824 | bytes 24122440 | solution.py:40
  193.1 6.5 scatter_fusion.5
  206.3 6.4 scatter_fusion.5
  213.7 26.3 %while.164 = (s32[]{:T(128)}, f32[8,128,256]{2,1,0:T(8,128)S(1)}, s32[2,32]{1,0:T(2,128)S(1)}, pred[2,32]{1,0:T(4,128)(4,1)S(1)}, bf16[2,32,128,128]{3,2,1,0:T(8...) while((s32[]{:T(128)}, f32[8,128,256]{2,1,0:T(8,128)S(1)}, ...), condition=%wide.region_20.21_spmd, body=%wide.region_18.20_spmd.sunk | while | flops 270533824 | bytes 24122440 | solution.py:40
  220.4 6.5 scatter_fusion.4
  233.6 6.5 scatter_fusion.4
  241.0 26.5 %while.163 = (s32[]{:T(128)}, f32[8,128,256]{2,1,0:T(8,128)S(1)}, s32[2,32]{1,0:T(2,128)S(1)}, pred[2,32]{1,0:T(4,128)(4,1)S(1)}, bf16[2,32,128,128]{3,2,1,0:T(8...) while((s32[]{:T(128)}, f32[8,128,256]{2,1,0:T(8,128)S(1)}, ...), condition=%wide.region_16.17_spmd, body=%wide.region_14.16_spmd.sunk | while | flops 270533824 | bytes 24122440 | solution.py:40
  247.9 6.5 scatter_fusion.3
  261.1 6.5 scatter_fusion.3
  268.6 26.3 %while.162 = (s32[]{:T(128)}, f32[8,128,256]{2,1,0:T(8,128)S(1)}, s32[2,32]{1,0:T(2,128)S(1)}, pred[2,32]{1,0:T(4,128)(4,1)S(1)}, bf16[2,32,128,128]{3,2,1,0:T(8...) while((s32[]{:T(128)}, f32[8,128,256]{2,1,0:T(8,128)S(1)}, ...), condition=%wide.region_12.13_spmd, body=%wide.region_10.12_spmd.sunk | while | flops 270533824 | bytes 24122440 | solution.py:40
  275.2 6.5 scatter_fusion.2
  288.4 6.5 scatter_fusion.2
  295.9 26.3 %while.160 = (s32[]{:T(128)}, f32[8,128,256]{2,1,0:T(8,128)S(1)}, s32[2,32]{1,0:T(2,128)S(1)}, pred[2,32]{1,0:T(4,128)(4,1)S(1)}, bf16[2,32,128,128]{3,2,1,0:T(8...) while((s32[]{:T(128)}, f32[8,128,256]{2,1,0:T(8,128)S(1)}, ...), condition=%wide.region_4.5_spmd, body=%wide.region_2.4_spmd.sunk | while | flops 270533824 | bytes 24122440 | solution.py:40
  302.6 6.5 scatter_fusion
  315.7 6.5 scatter_fusion
  323.5 34.7 %while.161 = (s32[]{:T(128)}, f32[8,128,256]{2,1,0:T(8,128)}, s32[2,32]{1,0:T(2,128)S(1)}, pred[2,32]{1,0:T(4,128)(4,1)S(1)}, bf16[2,32,128,128]{3,2,1,0:T(8,128...) while((s32[]{:T(128)}, f32[8,128,256]{2,1,0:T(8,128)}, s32[2,32]{1,0:T(2,128)S(1)}, ...), condition=%wide.region_8.9_spmd, body=%wide.region_6.8_spmd.sunk | while | flops 270533824 | bytes 24122440 | solution.py:40
  331.4 9.6 %scatter_fusion.1 = f32[8,128,256]{2,1,0:T(8,128)} fusion(f32[8,128,256]{2,1,0:T(8,128)} %get-tuple-element.1994, s32[32]{0:T(128)S(1)} %get-tuple-element.1689, f32[32,128,256]{2,1,0:T(8,128)} %convolution_select_fusion.33), kind=kCustom, calls=%fused_computation.17.clone.1 | custom fusion | flops 1048576 | bytes 12583040 | tf_op jit(solution)/shard_map/while/body/eval_jaxpr/scatter-add | solution.py:31
  348.7 9.5 %scatter_fusion.1 = f32[8,128,256]{2,1,0:T(8,128)} fusion(f32[8,128,256]{2,1,0:T(8,128)} %get-tuple-element.1994, s32[32]{0:T(128)S(1)} %get-tuple-element.1689, f32[32,128,256]{2,1,0:T(8,128)} %convolution_select_fusion.33), kind=kCustom, calls=%fused_computation.17.clone.1 | custom fusion | flops 1048576 | bytes 12583040 | tf_op jit(solution)/shard_map/while/body/eval_jaxpr/scatter-add | solution.py:31
  362.4 4.7 copy.27
  393.2 9.1 %all-reduce.6.cloned.1.call-done = f32[1024,256]{1,0:T(8,128)} async-done(((f32[1024,256]{1,0:T(8,128)}), f32[1024,256]{1,0:T(8,128)}) %all-reduce.6.cloned.1.call-update) | async-done | bytes 1048592 | tf_op jit(solution)/shard_map/psum | solution.py:93
  407.0 26.2 %while.168 = (s32[]{:T(128)}, f32[8,128,256]{2,1,0:T(8,128)S(1)}, s32[2,32]{1,0:T(2,128)S(1)}, pred[2,32]{1,0:T(4,128)(4,1)S(1)}, bf16[2,32,128,128]{2,3,1,0:T(8...) while((s32[]{:T(128)}, f32[8,128,256]{2,1,0:T(8,128)S(1)}, ...), condition=%wide.region_37.38_spmd, body=%wide.region_35.37_spmd.sunk | while | flops 270533824 | bytes 24122440 | solution.py:40
  413.7 6.4 scatter_fusion.8
  426.8 6.4 scatter_fusion.8
  434.4 26.3 %while.169 = (s32[]{:T(128)}, f32[8,128,256]{2,1,0:T(8,128)S(1)}, s32[2,32]{1,0:T(2,128)S(1)}, pred[2,32]{1,0:T(4,128)(4,1)S(1)}, bf16[2,32,128,128]{2,3,1,0:T(8...) while((s32[]{:T(128)}, f32[8,128,256]{2,1,0:T(8,128)S(1)}, ...), condition=%wide.region_40.41_spmd, body=%wide.region_38.40_spmd.sunk | while | flops 270533824 | bytes 24122440 | solution.py:40
  436.5 4.6 convolution_select_fusion.41
  441.1 6.4 scatter_fusion.9
  449.7 4.6 convolution_select_fusion.41
  454.3 6.4 scatter_fusion.9
  461.7 26.3 %while.170 = (s32[]{:T(128)}, f32[8,128,256]{2,1,0:T(8,128)S(1)}, s32[2,32]{1,0:T(2,128)S(1)}, pred[2,32]{1,0:T(4,128)(4,1)S(1)}, bf16[2,32,128,128]{2,3,1,0:T(8...) while((s32[]{:T(128)}, f32[8,128,256]{2,1,0:T(8,128)S(1)}, ...), condition=%wide.region_43.44_spmd, body=%wide.region_41.43_spmd.sunk | while | flops 270533824 | bytes 24122440 | solution.py:40
  463.8 4.6 convolution_select_fusion.42
  468.4 6.4 scatter_fusion.10
  481.6 6.4 scatter_fusion.10
  489.0 26.6 %while.171 = (s32[]{:T(128)}, f32[8,128,256]{2,1,0:T(8,128)S(1)}, s32[2,32]{1,0:T(2,128)S(1)}, pred[2,32]{1,0:T(4,128)(4,1)S(1)}, bf16[2,32,128,128]{2,3,1,0:T(8...) while((s32[]{:T(128)}, f32[8,128,256]{2,1,0:T(8,128)S(1)}, ...), condition=%wide.region_46.47_spmd, body=%wide.region_44.46_spmd.sunk | while | flops 270533824 | bytes 24122440 | solution.py:40
  491.3 4.6 convolution_select_fusion.43
  495.9 6.4 scatter_fusion.11
  504.5 4.6 convolution_select_fusion.43
  509.1 6.4 scatter_fusion.11
  516.5 26.3 %while.172 = (s32[]{:T(128)}, f32[8,128,256]{2,1,0:T(8,128)S(1)}, s32[2,32]{1,0:T(2,128)S(1)}, pred[2,32]{1,0:T(4,128)(4,1)S(1)}, bf16[2,32,128,128]{2,3,1,0:T(8...) while((s32[]{:T(128)}, f32[8,128,256]{2,1,0:T(8,128)S(1)}, ...), condition=%wide.region_49.50_spmd, body=%wide.region_47.49_spmd.sunk | while | flops 270533824 | bytes 24122440 | solution.py:40
  523.3 6.4 scatter_fusion.12
  531.8 4.6 convolution_select_fusion.44
  536.4 6.4 scatter_fusion.12
  543.9 26.2 %while.173 = (s32[]{:T(128)}, f32[8,128,256]{2,1,0:T(8,128)S(1)}, s32[2,32]{1,0:T(2,128)S(1)}, pred[2,32]{1,0:T(4,128)(4,1)S(1)}, bf16[2,32,128,128]{2,3,1,0:T(8...) while((s32[]{:T(128)}, f32[8,128,256]{2,1,0:T(8,128)S(1)}, ...), condition=%wide.region_52.53_spmd, body=%wide.region_50.52_spmd.sunk | while | flops 270533824 | bytes 24122440 | solution.py:40
  550.6 6.4 scatter_fusion.13
  563.7 6.4 scatter_fusion.13
  571.1 26.3 %while.174 = (s32[]{:T(128)}, f32[8,128,256]{2,1,0:T(8,128)S(1)}, s32[2,32]{1,0:T(2,128)S(1)}, pred[2,32]{1,0:T(4,128)(4,1)S(1)}, bf16[2,32,128,128]{2,3,1,0:T(8...) while((s32[]{:T(128)}, f32[8,128,256]{2,1,0:T(8,128)S(1)}, ...), condition=%wide.region_55.56_spmd, body=%wide.region_53.55_spmd.sunk | while | flops 270533824 | bytes 24122440 | solution.py:40
  577.8 6.4 scatter_fusion.14
  586.3 4.6 convolution_select_fusion.46
  590.9 6.4 scatter_fusion.14
  598.5 26.2 %while.175 = (s32[]{:T(128)}, f32[8,128,256]{2,1,0:T(8,128)S(1)}, s32[2,32]{1,0:T(2,128)S(1)}, pred[2,32]{1,0:T(4,128)(4,1)S(1)}, bf16[2,32,128,128]{2,3,1,0:T(8...) while((s32[]{:T(128)}, f32[8,128,256]{2,1,0:T(8,128)S(1)}, ...), condition=%wide.region_58.59_spmd, body=%wide.region_56.58_spmd.sunk | while | flops 270533824 | bytes 24122440 | solution.py:40
  605.2 6.4 scatter_fusion.15
  613.6 4.6 convolution_select_fusion.47
  618.2 6.4 scatter_fusion.15
  632.8 8.0 fusion.113
  643.7 101.9 %reduce-scatter.2.cloned.1.call-done = f32[512,256]{1,0:T(8,128)} async-done(((f32[8192,256]{1,0:T(8,128)}), f32[512,256]{1,0:T(8,128)}) %reduce-scatter.2.cloned.1.call-update) | async-done | bytes 524304 | tf_op jit(solution)/shard_map/reduce_scatter | solution.py:130
  747.4 128.9 %all-reduce.8.cloned.1.call-done = f32[256,256]{1,0:T(8,128)} async-done(((f32[256,256]{1,0:T(8,128)}), f32[256,256]{1,0:T(8,128)}) %all-reduce.8.cloned.1.call-update) | async-done | bytes 262160 | tf_op jit(solution)/shard_map/psum | solution.py:110
  (450 shorter events, 267.7 us)
Async XLA Ops:
  7.2 396.6 %copy-start = (bf16[256,256]{1,0:T(8,128)(2,1)S(1)}, bf16[256,256]{1,0:T(8,128)(2,1)}, u32[]{:S(2)}) copy-start(bf16[256,256]{1,0:T(8,128)(2,1)} %param.42) | copy-start | bytes 393220
  7.2 122.3 %all-reduce.10.cloned.1.call-start = ((), (), s32[]{:S(2)}) async-start(), calls=%async_computation.4 | async-start | bytes 8388608 | tf_op jit(solution)/shard_map/psum | solution.py:9
  8.0 3.3 copy-start.43
  11.4 6.7 copy-start.75
  11.4 6.7 copy-start.76
  11.4 390.9 %all-reduce.6.cloned.1.call-start = ((), (), s32[]{:S(2)}) async-start(), calls=%async_computation.1 | async-start | bytes 2097152 | tf_op jit(solution)/shard_map/psum | solution.py:93
  129.6 29.1 %copy-start.29 = (bf16[8,128,256]{2,1,0:T(8,128)(2,1)S(1)}, bf16[8,128,256]{2,1,0:T(8,128)(2,1)}, u32[]{:S(2)}) copy-start(bf16[8,128,256]{2,1,0:T(8,128)(2,1)} %get-tuple-element.1847) | copy-start | bytes 1572868
  158.7 26.7 %copy-start.28 = (bf16[8,128,256]{2,1,0:T(8,128)(2,1)S(1)}, bf16[8,128,256]{2,1,0:T(8,128)(2,1)}, u32[]{:S(2)}) copy-start(bf16[8,128,256]{2,1,0:T(8,128)(2,1)} %get-tuple-element.1871) | copy-start | bytes 1572868
  185.5 27.4 %copy-start.27 = (bf16[8,128,256]{2,1,0:T(8,128)(2,1)S(1)}, bf16[8,128,256]{2,1,0:T(8,128)(2,1)}, u32[]{:S(2)}) copy-start(bf16[8,128,256]{2,1,0:T(8,128)(2,1)} %get-tuple-element.1895) | copy-start | bytes 1572868
  212.9 27.3 %copy-start.26 = (bf16[8,128,256]{2,1,0:T(8,128)(2,1)S(1)}, bf16[8,128,256]{2,1,0:T(8,128)(2,1)}, u32[]{:S(2)}) copy-start(bf16[8,128,256]{2,1,0:T(8,128)(2,1)} %get-tuple-element.1919) | copy-start | bytes 1572868
  240.2 27.5 %copy-start.25 = (bf16[8,128,256]{2,1,0:T(8,128)(2,1)S(1)}, bf16[8,128,256]{2,1,0:T(8,128)(2,1)}, u32[]{:S(2)}) copy-start(bf16[8,128,256]{2,1,0:T(8,128)(2,1)} %get-tuple-element.1943) | copy-start | bytes 1572868
  240.2 27.5 %copy-start.67 = (s32[2,32]{1,0:T(2,128)S(1)}, s32[2,32]{1,0:T(2,128)}, u32[]{:S(2)}) copy-start(s32[2,32]{1,0:T(2,128)} %reshape.1266) | copy-start | bytes 772
  240.2 27.5 %copy-start.69 = (s32[2,32]{1,0:T(2,128)S(1)}, s32[2,32]{1,0:T(2,128)}, u32[]{:S(2)}) copy-start(s32[2,32]{1,0:T(2,128)} %min.110) | copy-start | bytes 772
  240.2 27.5 %copy-start.94 = (pred[2,32]{1,0:T(4,128)(4,1)S(1)}, pred[2,32]{1,0:T(4,128)(4,1)}, u32[]{:S(2)}) copy-start(pred[2,32]{1,0:T(4,128)(4,1)} %compare_and_fusion.5) | copy-start | bytes 196
  267.8 27.2 %copy-start.24 = (bf16[8,128,256]{2,1,0:T(8,128)(2,1)S(1)}, bf16[8,128,256]{2,1,0:T(8,128)(2,1)}, u32[]{:S(2)}) copy-start(bf16[8,128,256]{2,1,0:T(8,128)(2,1)} %get-tuple-element.1967) | copy-start | bytes 1572868
  267.8 27.2 %copy-start.73 = (s32[2,32]{1,0:T(2,128)S(1)}, s32[2,32]{1,0:T(2,128)}, u32[]{:S(2)}) copy-start(s32[2,32]{1,0:T(2,128)} %reshape.1260) | copy-start | bytes 772
  267.8 27.2 %copy-start.74 = (s32[2,32]{1,0:T(2,128)S(1)}, s32[2,32]{1,0:T(2,128)}, u32[]{:S(2)}) copy-start(s32[2,32]{1,0:T(2,128)} %min.104) | copy-start | bytes 772
  267.8 27.2 %copy-start.97 = (pred[2,32]{1,0:T(4,128)(4,1)S(1)}, pred[2,32]{1,0:T(4,128)(4,1)}, u32[]{:S(2)}) copy-start(pred[2,32]{1,0:T(4,128)(4,1)} %compare_and_fusion.7) | copy-start | bytes 196
  295.0 28.5 %copy-start.71 = (s32[2,32]{1,0:T(2,128)S(1)}, s32[2,32]{1,0:T(2,128)}, u32[]{:S(2)}) copy-start(s32[2,32]{1,0:T(2,128)} %reshape.1263) | copy-start | bytes 772
  295.0 28.5 %copy-start.72 = (s32[2,32]{1,0:T(2,128)S(1)}, s32[2,32]{1,0:T(2,128)}, u32[]{:S(2)}) copy-start(s32[2,32]{1,0:T(2,128)} %min.107) | copy-start | bytes 772
  295.0 28.5 %copy-start.96 = (pred[2,32]{1,0:T(4,128)(4,1)S(1)}, pred[2,32]{1,0:T(4,128)(4,1)}, u32[]{:S(2)}) copy-start(pred[2,32]{1,0:T(4,128)(4,1)} %compare_and_fusion.6) | copy-start | bytes 196
  323.5 34.7 %copy-start.3 = (f32[8,128,256]{2,1,0:T(8,128)S(1)}, f32[8,128,256]{2,1,0:T(8,128)}, u32[]{:S(2)}) copy-start(f32[8,128,256]{2,1,0:T(8,128)} %copy-done.2) | copy-start | bytes 3145732
  323.5 34.7 %copy-start.5 = (f32[8,128,256]{2,1,0:T(8,128)S(1)}, f32[8,128,256]{2,1,0:T(8,128)}, u32[]{:S(2)}) copy-start(f32[8,128,256]{2,1,0:T(8,128)} %copy-done.4) | copy-start | bytes 3145732
  323.5 34.7 %copy-start.7 = (f32[8,128,256]{2,1,0:T(8,128)S(1)}, f32[8,128,256]{2,1,0:T(8,128)}, u32[]{:S(2)}) copy-start(f32[8,128,256]{2,1,0:T(8,128)} %copy-done.6) | copy-start | bytes 3145732
  358.3 4.1 copy-start.45
  358.3 4.1 copy-start.83
  362.3 383.3 %reduce-scatter.2.cloned.1.call-start = ((), (), s32[]{:S(2)}) async-start(), calls=%async_computation.3 | async-start | bytes 8912896 | tf_op jit(solution)/shard_map/reduce_scatter | solution.py:130
  362.4 4.7 copy-start.33
  370.1 4.3 copy-start.32
  377.3 4.2 copy-start.31
  384.5 4.2 copy-start.30
  388.7 3.0 copy-start.82
  388.7 3.0 copy-start.81
  388.7 3.0 copy-start.80
  388.7 3.1 copy-start.79
  388.7 3.1 copy-start.78
  388.7 3.1 copy-start.77
  388.7 13.6 %copy-start.35 = (bf16[1024,256]{1,0:T(8,128)(2,1)S(1)}, bf16[1024,256]{1,0:T(8,128)(2,1)}, u32[]{:S(2)}) copy-start(bf16[1024,256]{1,0:T(8,128)(2,1)} %param.40) | copy-start | bytes 1572868
  388.8 13.6 %copy-start.44 = (f32[1024]{0:T(1024)S(1)}, f32[1024]{0:T(1024)}, u32[]{:S(2)}) copy-start(f32[1024]{0:T(1024)} %copy-done.43) | copy-start | bytes 12292
  391.7 12.1 %copy-start.98 = (bf16[1024,256]{1,0:T(8,128)(2,1)S(1)}, bf16[1024,256]{1,0:T(8,128)(2,1)}, u32[]{:S(2)}) copy-start(bf16[1024,256]{1,0:T(8,128)(2,1)} %param.47) | copy-start | bytes 1572868
  434.4 26.5 %copy-start.68 = (s32[2,32]{1,0:T(2,128)S(1)}, s32[2,32]{1,0:T(2,128)}, u32[]{:S(2)}) copy-start(s32[2,32]{1,0:T(2,128)} %reshape.1266) | copy-start | bytes 772
  434.4 26.5 %copy-start.70 = (s32[2,32]{1,0:T(2,128)S(1)}, s32[2,32]{1,0:T(2,128)}, u32[]{:S(2)}) copy-start(s32[2,32]{1,0:T(2,128)} %min.110) | copy-start | bytes 772
  434.4 26.5 %copy-start.95 = (pred[2,32]{1,0:T(4,128)(4,1)S(1)}, pred[2,32]{1,0:T(4,128)(4,1)}, u32[]{:S(2)}) copy-start(pred[2,32]{1,0:T(4,128)(4,1)} %compare_and_fusion.5) | copy-start | bytes 196
  460.9 27.2 %copy-start.64 = (s32[2,32]{1,0:T(2,128)S(1)}, s32[2,32]{1,0:T(2,128)}, u32[]{:S(2)}) copy-start(s32[2,32]{1,0:T(2,128)} %copy-done.63) | copy-start | bytes 772
  460.9 27.2 %copy-start.66 = (s32[2,32]{1,0:T(2,128)S(1)}, s32[2,32]{1,0:T(2,128)}, u32[]{:S(2)}) copy-start(s32[2,32]{1,0:T(2,128)} %copy-done.65) | copy-start | bytes 772
  460.9 27.2 %copy-start.93 = (pred[2,32]{1,0:T(4,128)(4,1)S(1)}, pred[2,32]{1,0:T(4,128)(4,1)}, u32[]{:S(2)}) copy-start(pred[2,32]{1,0:T(4,128)(4,1)} %copy-done.92) | copy-start | bytes 196
  488.1 27.6 %copy-start.60 = (s32[2,32]{1,0:T(2,128)S(1)}, s32[2,32]{1,0:T(2,128)}, u32[]{:S(2)}) copy-start(s32[2,32]{1,0:T(2,128)} %copy-done.59) | copy-start | bytes 772
  488.1 27.6 %copy-start.62 = (s32[2,32]{1,0:T(2,128)S(1)}, s32[2,32]{1,0:T(2,128)}, u32[]{:S(2)}) copy-start(s32[2,32]{1,0:T(2,128)} %copy-done.61) | copy-start | bytes 772
  488.1 27.6 %copy-start.91 = (pred[2,32]{1,0:T(4,128)(4,1)S(1)}, pred[2,32]{1,0:T(4,128)(4,1)}, u32[]{:S(2)}) copy-start(pred[2,32]{1,0:T(4,128)(4,1)} %copy-done.90) | copy-start | bytes 196
  515.7 27.3 %copy-start.56 = (s32[2,32]{1,0:T(2,128)S(1)}, s32[2,32]{1,0:T(2,128)}, u32[]{:S(2)}) copy-start(s32[2,32]{1,0:T(2,128)} %copy-done.55) | copy-start | bytes 772
  515.7 27.3 %copy-start.58 = (s32[2,32]{1,0:T(2,128)S(1)}, s32[2,32]{1,0:T(2,128)}, u32[]{:S(2)}) copy-start(s32[2,32]{1,0:T(2,128)} %copy-done.57) | copy-start | bytes 772
  515.7 27.3 %copy-start.89 = (pred[2,32]{1,0:T(4,128)(4,1)S(1)}, pred[2,32]{1,0:T(4,128)(4,1)}, u32[]{:S(2)}) copy-start(pred[2,32]{1,0:T(4,128)(4,1)} %copy-done.88) | copy-start | bytes 196
  543.0 27.2 %copy-start.52 = (s32[2,32]{1,0:T(2,128)S(1)}, s32[2,32]{1,0:T(2,128)}, u32[]{:S(2)}) copy-start(s32[2,32]{1,0:T(2,128)} %copy-done.51) | copy-start | bytes 772
  543.0 27.2 %copy-start.54 = (s32[2,32]{1,0:T(2,128)S(1)}, s32[2,32]{1,0:T(2,128)}, u32[]{:S(2)}) copy-start(s32[2,32]{1,0:T(2,128)} %copy-done.53) | copy-start | bytes 772
  543.0 27.2 %copy-start.87 = (pred[2,32]{1,0:T(4,128)(4,1)S(1)}, pred[2,32]{1,0:T(4,128)(4,1)}, u32[]{:S(2)}) copy-start(pred[2,32]{1,0:T(4,128)(4,1)} %copy-done.86) | copy-start | bytes 196
  570.2 28.2 %copy-start.48 = (s32[2,32]{1,0:T(2,128)S(1)}, s32[2,32]{1,0:T(2,128)}, u32[]{:S(2)}) copy-start(s32[2,32]{1,0:T(2,128)} %copy-done.47) | copy-start | bytes 772
  570.3 28.2 %copy-start.50 = (s32[2,32]{1,0:T(2,128)S(1)}, s32[2,32]{1,0:T(2,128)}, u32[]{:S(2)}) copy-start(s32[2,32]{1,0:T(2,128)} %copy-done.49) | copy-start | bytes 772
  570.3 28.2 %copy-start.85 = (pred[2,32]{1,0:T(4,128)(4,1)S(1)}, pred[2,32]{1,0:T(4,128)(4,1)}, u32[]{:S(2)}) copy-start(pred[2,32]{1,0:T(4,128)(4,1)} %copy-done.84) | copy-start | bytes 196
  598.5 26.2 %copy-start.13 = (f32[8,128,256]{2,1,0:T(8,128)S(1)}, f32[8,128,256]{2,1,0:T(8,128)}, u32[]{:S(2)}) copy-start(f32[8,128,256]{2,1,0:T(8,128)} %copy-done.12) | copy-start | bytes 3145732
  624.7 2.6 copy-start.17
  630.6 2.2 copy-start.42
  630.6 2.2 copy-start.46
  640.8 237.2 %copy-start.1 = (bf16[256,256]{1,0:T(8,128)(2,1)S(1)}, bf16[256,256]{1,0:T(8,128)(2,1)}, u32[]{:S(2)}) copy-start(bf16[256,256]{1,0:T(8,128)(2,1)} %param.42) | copy-start | bytes 393220
  640.8 235.5 %all-reduce.8.cloned.1.call-start = ((), (), s32[]{:S(2)}) async-start(), calls=%async_computation.2 | async-start | bytes 524288 | tf_op jit(solution)/shard_map/psum | solution.py:110
  (40 other events, 47.8 us)
Sparse Core Ops, SparseCore 0:
  12.6 116.8 all-reduce.9
  362.5 39.8 all-reduce.5
  640.9 104.6 reduce-scatter.1
  751.5 124.7 all-reduce.7
where the time goes:
time: 897 us; the launch traced here: 885 us
  waiting for transfers between devices  257 us (29%)
  other arithmetic  246 us (27%)
  matrix products  151 us (17%)
  local copies, waits for them, and re-layouts  144 us (16%)
  blocking collectives  64.5 us (7%)
  between operations  20.6 us (2%)
    scatter-add x32, other arithmetic, advance(): return (carry.at[out_block].add(prod), None)  212 us
    psum x1, waiting for transfers between devices, shards(): weight_grad = lax.psum(local_grad * grad_factor, ('rows', 'rep'))  129 us
    reduce_scatter x1, waiting for transfers between devices, shards(): lax.psum_scatter(terms.reshape(sections * nodes_block, width), 'rows', sc...  102 us
    dot_general x16, matrix products, advance(): jnp.einsum('kji,kjf->kif', vals_block, picked, preferred_element_type=jnp...  74 us
    dot_general x16, matrix products, advance(): jnp.einsum('kij,kjf->kif', vals_block, picked, preferred_element_type=jnp...  73.4 us
    gather x32, local copies, waits for them, and re-layouts, advance(): picked = source[in_block]  70 us
    psum x1, blocking collectives, from_root(): return lax.psum(jnp.where(mine, shard, jnp.zeros_like(shard)), axis)  64.5 us
    dynamic_slice x9, local copies, waits for them, and re-layouts, section_window(): vals_window = lax.dynamic_slice_in_dim(values, first, pair_slots, 0)  41.3 us
  transfers between devices with their start and end apart: 4, of which 4 were waited for; matrix products, arithmetic and copies ran while one was open for 7% of the time, Pallas kernels for 0%

commit v1 on v0

v1 whole, which is shorter than its diff:
```python
import functools

import jax
import jax.numpy as jnp
from jax import lax
from jax.experimental import pallas as pl
from jax.experimental.pallas import tpu as pltpu
from jax.sharding import PartitionSpec as P

LIMIT = 48 * 2**20


def densify_kernel(per_block, starts, ends, rows, cols, vals_ref, dense_ref):
    section = pl.program_id(0)
    tile = vals_ref.shape[-1]
    dense_ref[...] = jnp.zeros_like(dense_ref)

    def place(slot, carry):
        row = pl.multiple_of(rows[slot] * tile, tile)
        col = pl.multiple_of((cols[slot] - section * per_block) * tile, tile)
        dense_ref[pl.ds(row, tile), pl.ds(col, tile)] = vals_ref[slot]
        return carry

    lax.fori_loop(starts[section], ends[section], place, 0)


def densify(values, rows, cols, starts, ends, per_block, sections):
    slots, tile, _ = values.shape
    block = per_block * tile
    return pl.pallas_call(
        functools.partial(densify_kernel, per_block),
        out_shape=jax.ShapeDtypeStruct((block, sections * block), values.dtype),
        grid_spec=pltpu.PrefetchScalarGridSpec(
            num_scalar_prefetch=4,
            grid=(sections,),
            in_specs=[pl.BlockSpec((slots, tile, tile), lambda s, *_: (0, 0, 0))],
            out_specs=pl.BlockSpec((block, block), lambda s, *_: (0, s)),
        ),
        compiler_params=pltpu.CompilerParams(vmem_limit_bytes=LIMIT),
        cost_estimate=pl.CostEstimate(
            flops=0, bytes_accessed=2 * (slots * tile * tile + block * sections * block), transcendentals=0
        ),
        name="densify",
    )(starts, ends, rows, cols, values)


def forward_kernel(dense_ref, source_ref, total_ref, sent_ref):
    section = pl.program_id(0)
    part = jnp.dot(dense_ref[...], source_ref[...], preferred_element_type=jnp.float32)

    @pl.when(section == 0)
    def _():
        total_ref[...] = part

    @pl.when(section > 0)
    def _():
        total_ref[...] += part

    @pl.when(section == pl.num_programs(0) - 1)
    def _():
        sent_ref[...] = total_ref[...].astype(sent_ref.dtype)


def forward(dense, source, sections):
    block, depth = dense.shape
    width = source.shape[-1]
    step = depth // sections
    return pl.pallas_call(
        forward_kernel,
        out_shape=(
            jax.ShapeDtypeStruct((block, width), jnp.float32),
            jax.ShapeDtypeStruct((block, width), jnp.bfloat16),
        ),
        grid=(sections,),
        in_specs=[
            pl.BlockSpec((block, step), lambda s: (0, s)),
            pl.BlockSpec((step, width), lambda s: (s, 0)),
        ],
        out_specs=(
            pl.BlockSpec((block, width), lambda s: (0, 0)),
            pl.BlockSpec((block, width), lambda s: (0, 0)),
        ),
        compiler_params=pltpu.CompilerParams(vmem_limit_bytes=LIMIT),
        cost_estimate=pl.CostEstimate(
            flops=2 * block * depth * width,
            bytes_accessed=2 * (block * depth + depth * width) + 6 * block * width,
            transcendentals=0,
        ),
        name="forward_product",
    )(dense, source)


def middle_kernel(
    share, factor, replica, own_ref, other_ref, feats_ref, deg_col_ref, deg_row_ref, weight_ref,
    cot_ref, act_ref, grad_ref, back_ref, prop_ref, pre_ref, full_ref,
):
    degree = deg_col_ref[...]
    scaled = (degree * feats_ref[...].astype(jnp.float32)).astype(jnp.bfloat16)
    summed = own_ref[...] + other_ref[...].astype(jnp.float32)
    propagated = (degree * (summed + scaled.astype(jnp.float32))).astype(jnp.bfloat16)
    weight = weight_ref[...]
    preact = jnp.dot(propagated, weight, preferred_element_type=jnp.float32)
    gate = jax.nn.sigmoid(preact)
    full_ref[...] = (preact * gate).astype(jnp.bfloat16)
    grad_pre = (cot_ref[...].astype(jnp.float32) * gate * (1.0 + preact * (1.0 - gate))).astype(
        jnp.bfloat16
    )
    prop_ref[...] = propagated
    pre_ref[...] = grad_pre
    spread = lax.dot_general(
        weight, grad_pre, (((1,), (1,)), ((), ())), preferred_element_type=jnp.float32
    )
    back_ref[...] = (deg_row_ref[...] * spread).astype(jnp.bfloat16)
    mine = pl.ds(pl.multiple_of(replica[0] * share, share), share)
    act_ref[...] = full_ref[mine, :]
    grad_ref[...] = factor * lax.dot_general(
        prop_ref[mine, :], pre_ref[mine, :], (((0,), (0,)), ((), ())),
        preferred_element_type=jnp.float32,
    )


def middle(replica, own, other, features, degree, weight, cotangent, share, factor):
    block, width = features.shape
    vmem = pl.BlockSpec(memory_space=pltpu.VMEM)
    return pl.pallas_call(
        functools.partial(middle_kernel, share, factor),
        out_shape=(
            jax.ShapeDtypeStruct((share, width), jnp.bfloat16),
            jax.ShapeDtypeStruct((width, width), jnp.float32),
            jax.ShapeDtypeStruct((width, block), jnp.bfloat16),
        ),
        in_specs=[pl.BlockSpec(memory_space=pltpu.SMEM)] + [vmem] * 7,
        out_specs=(vmem, vmem, vmem),
        scratch_shapes=[pltpu.VMEM((block, width), jnp.bfloat16)] * 3,
        compiler_params=pltpu.CompilerParams(vmem_limit_bytes=LIMIT),
        cost_estimate=pl.CostEstimate(
            flops=5 * block * width * width, bytes_accessed=16 * block * width, transcendentals=block * width
        ),
        name="middle",
    )(
        replica.reshape(1), own, other, features, degree.reshape(block, 1), degree.reshape(1, block),
        weight, cotangent,
    )


def backward_kernel(own_section, back_ref, dense_ref, out_ref):
    section = pl.program_id(0)
    back = back_ref[...]
    part = jnp.dot(back, dense_ref[...], preferred_element_type=jnp.float32)
    mine = (section == own_section[0]).astype(jnp.float32)
    part = (part + mine * back.astype(jnp.float32)).astype(out_ref.dtype)
    shares, _, share = out_ref.shape
    for piece in range(shares):
        out_ref[piece] = part[:, piece * share : (piece + 1) * share]


def backward(own_section, back, dense, sections, shares):
    width, block = back.shape
    depth = dense.shape[1]
    step = depth // sections
    share = step // shares
    return pl.pallas_call(
        backward_kernel,
        out_shape=jax.ShapeDtypeStruct((sections * shares, width, share), jnp.bfloat16),
        grid_spec=pltpu.PrefetchScalarGridSpec(
            num_scalar_prefetch=1,
            grid=(sections,),
            in_specs=[
                pl.BlockSpec((width, block), lambda s, *_: (0, 0)),
                pl.BlockSpec((block, step), lambda s, *_: (0, s)),
            ],
            out_specs=pl.BlockSpec((shares, width, share), lambda s, *_: (s, 0, 0)),
        ),
        compiler_params=pltpu.CompilerParams(vmem_limit_bytes=LIMIT),
        cost_estimate=pl.CostEstimate(
            flops=2 * block * depth * width,
            bytes_accessed=2 * (block * depth + depth * width + block * width),
            transcendentals=0,
        ),
        name="backward_product",
    )(own_section.reshape(1), back, dense)


def shards(features, inv_sqrt_degree, weight, tile_vals, tile_row, tile_col, tile_count, cotangent):
    rows_count = lax.axis_size("rows")
    rep_count = lax.axis_size("rep")
    sections = rows_count // rep_count
    replica = lax.axis_index("rep").astype(jnp.int32)
    block_row = lax.axis_index("rows").astype(jnp.int32)
    nodes_block, width = features.shape
    tile = tile_vals.shape[-1]
    per_block = nodes_block // tile
    share = nodes_block // rep_count
    counts = tile_count[0]
    ends = jnp.cumsum(counts).astype(jnp.int32)
    starts = ends - counts
    degree = inv_sqrt_degree.astype(jnp.float32)
    grad_factor = float(nodes_block * rows_count) ** (-0.5)

    route = []
    for row in range(rows_count):
        for rep in range(rep_count):
            goal_row = (row % sections) * rep_count + rep
            goal_rep = row // sections
            route.append((row * rep_count + rep, goal_row * rep_count + goal_rep))
    part_feats = lax.dynamic_slice_in_dim(features, replica * share, share, 0)
    part_degree = lax.dynamic_slice_in_dim(degree, replica * share, share, 0)
    part_scaled = (part_degree[:, None] * part_feats.astype(jnp.float32)).astype(jnp.bfloat16)
    placed = lax.ppermute(part_scaled, ("rows", "rep"), route)
    placed_degree = lax.ppermute(part_degree, ("rows", "rep"), route)
    source = lax.all_gather(placed, "rows", axis=0, tiled=True)

    dense = densify(tile_vals[0], tile_row[0], tile_col[0], starts, ends, per_block, sections)
    own, sent = forward(dense, source, sections)
    if rep_count == 2:
        other = lax.ppermute(sent, "rep", [(0, 1), (1, 0)])
    else:
        other = lax.psum(own, "rep") - own
    activated, local_grad, back = middle(
        replica, own, other, features, degree, weight, cotangent, share, grad_factor
    )
    weight_grad = lax.psum(local_grad, ("rows", "rep"))
    terms = backward(block_row - replica * sections, back, dense, sections, rep_count)
    gathered = lax.psum_scatter(terms, "rows", scatter_dimension=0, tiled=False)
    feature_grad = (placed_degree[:, None] * gathered.astype(jnp.float32).T).astype(jnp.bfloat16)
    return (activated, weight_grad, feature_grad)


def solution(mesh):
    placed = (
        P("rows", None),
        P("rows"),
        P(),
        P("rows", "rep", None, None),
        P("rows", "rep"),
        P("rows", "rep"),
        P("rows", "rep"),
        P("rows", None),
    )
    return jax.shard_map(
        shards,
        mesh=mesh,
        in_specs=placed,
        out_specs=(P(("rows", "rep"), None), P(), P(("rep", "rows"), None)),
        check_vma=False,
    )
```

time: 897 us -> 327 us (0.36); the launches traced: 885 us -> 327 us
  other arithmetic: 246 us -> 3.57 us
  matrix products: 151 us -> 0 us
  local copies, waits for them, and re-layouts: 144 us -> 9.69 us
  blocking collectives: 64.5 us -> 0 us
  Pallas kernels: 0 us -> 35 us
    scatter-add x32 -> x0, other arithmetic: 212 us -> none  [advance(): return (carry.at[out_block].add(prod), None)]
    dot_general x35 -> x0, matrix products: 151 us -> none  [the longest x16 74 us: advance(): jnp.einsum('kji,kjf->kif', vals_block, picked, preferred_element_type=jnp...]
    gather x32 -> x0, local copies, waits for them, and re-layouts: 70 us -> none  [advance(): picked = source[in_block]]
    psum x1 -> x0, blocking collectives: 64.5 us -> none  [from_root(): return lax.psum(jnp.where(mine, shard, jnp.zeros_like(shard)), axis)]
    all_gather x0 -> x1, waiting for transfers between devices: none -> 49.7 us  [shards(): source = lax.all_gather(placed, 'rows', axis=0, tiled=True)]
    dynamic_slice x9 -> x1, local copies, waits for them, and re-layouts: 41.3 us -> 0.76 us  [shards(): part_degree = lax.dynamic_slice_in_dim(degree, replica * share, share, 0)]
    pallas_call x0 -> x4, Pallas kernels: none -> 35 us  [the longest x1 11.8 us: forward(): pl.pallas_call(forward_kernel, out_shape=(jax.ShapeDtypeStruct((block, wi...]
    reduce_scatter x1, waiting for transfers between devices: 102 us -> 70.2 us  [shards(): gathered = lax.psum_scatter(terms, 'rows', scatter_dimension=0, tiled=False)]
  transfers between devices with their start and end apart: 4 -> 6, of which waited for: 4 -> 4; matrix products, arithmetic and copies ran while one was open for 7% -> 1% of each run, Pallas kernels for 0% -> 3%
where the time goes in v1:
time: 327 us
  waiting for transfers between devices  262 us (80%)
  Pallas kernels  35 us (11%)
  between operations  13.8 us (4%)
  local copies, waits for them, and re-layouts  9.69 us (3%)
  other arithmetic  3.57 us (1%)
    psum x1, waiting for transfers between devices, shards(): weight_grad = lax.psum(local_grad, ('rows', 'rep'))  129 us
    reduce_scatter x1, waiting for transfers between devices, shards(): gathered = lax.psum_scatter(terms, 'rows', scatter_dimension=0, tiled=False)  70.2 us
    all_gather x1, waiting for transfers between devices, shards(): source = lax.all_gather(placed, 'rows', axis=0, tiled=True)  49.7 us
    ppermute x1, waiting for transfers between devices, shards(): other = lax.ppermute(sent, 'rep', [(0, 1), (1, 0)])  12.6 us
    pallas_call x1, Pallas kernels, forward(): pl.pallas_call(forward_kernel, out_shape=(jax.ShapeDtypeStruct((block, wi...  11.8 us
    pallas_call x1, Pallas kernels, densify(): pl.pallas_call(functools.partial(densify_kernel, per_block), out_shape=ja...  11 us
    pallas_call x1, Pallas kernels, backward(): pl.pallas_call(backward_kernel, out_shape=jax.ShapeDtypeStruct((sections...  10.4 us
    unnamed x20, local copies, waits for them, and re-layouts  8.71 us
  transfers between devices with their start and end apart: 6, of which 4 were waited for; matrix products, arithmetic and copies ran while one was open for 1% of the time, Pallas kernels for 3%

profile of v1, /device:TPU:0, one launch (start us, length us, event | category | flops | bytes accessed | tf_op | source)
XLA Modules:
  0.0 326.8 jit_solution(9648998969486930806)
XLA Ops:
  7.2 0.0 all-gather.2.cloned.1.call-start
  7.2 0.8 dynamic_slice.6
  8.0 1.1 multiply_convert_fusion
  9.1 0.7 collective-permute-start
  9.7 0.0 collective-permute-done
  9.8 0.0 copy-start.7
  9.8 0.7 copy-done.7
  10.5 0.0 all-gather.2.cloned.1.call-update
  10.5 0.0 reduce-scatter.2.cloned.1.call-start
  10.5 0.8 reduce-window.9
  11.4 0.7 bitcast_subtract_fusion.starts
  12.0 0.0 copy-start.5
  12.0 0.7 copy-done.5
  12.7 0.0 copy-start.6
  12.7 0.7 copy-done.6
  13.4 11.0 %densify.1.dense_ref = bf16[1024,8192]{1,0:T(8,128)(2,1)} custom-call(s32[8]{0:T(128)S(1)} %bitcast_subtract_fusion.starts, s32[8]{0:T(128)S(1)} %bitcast.21, s32[256]{0:T(256)S(1)} %bitcast.19, s32[256]{0:T(256)S(1)} %bitcast.20, bf16[256,128,128]{2,1,0:T(8,128)(2,1)} %bitcast.22), custom_call_target="tpu_custom_call" | custom-call | bytes 25165824 | tf_op jit(solution)/shard_map/densify/pallas_call | solution.py:30
  24.4 49.7 %all-gather.2.cloned.1.call-done.source_ref = bf16[8192,256]{1,0:T(8,128)(2,1)} async-done(((bf16[512,256]{1,0:T(8,128)(2,1)}), bf16[8192,256]{1,0:T(8,128)(2,1)}) %all-gather.2.cloned.1.call-update) | async-done | bytes 4194320 | tf_op jit(solution)/shard_map/all_gather | solution.py:211
  74.1 0.0 copy-start.1
  74.1 2.2 copy-done.1
  76.3 0.0 copy-start.8
  76.3 0.0 copy-start.2
  76.3 0.0 copy-start.3
  76.3 0.0 copy-start.4
  76.3 11.8 %forward_product.1 = (f32[1024,256]{1,0:T(8,128)S(1)}, bf16[1024,256]{1,0:T(8,128)(2,1)}) custom-call(bf16[1024,8192]{1,0:T(8,128)(2,1)} %densify.1.dense_ref, bf16[8192,256]{1,0:T(8,128)(2,1)S(1)} %copy-done.1), custom_call_target="tpu_custom_call" | custom-call | flops 4294967296 | bytes 22544384 | tf_op jit(solution)/shard_map/forward_product/pallas_call | solution.py:68
  88.1 1.5 collective-permute-start.1
  89.6 0.0 copy-done.8
  89.6 0.2 copy.12.deg_col_ref
  89.8 12.6 %collective-permute-done.1.other_ref = bf16[1024,256]{1,0:T(8,128)(2,1)S(1)} collective-permute-done((bf16[1024,256]{1,0:T(8,128)(2,1)}, bf16[1024,256]{1,0:T(8,128)(2,1)S(1)}, u32[]{:S(2)}, u32[]{:S(2)}) %collective-permute-start.1) | collective-permute-done | bytes 524320 | tf_op jit(solution)/shard_map/ppermute | solution.py:216
  102.4 0.0 copy-done.2
  102.4 0.0 copy-done.3
  102.4 0.0 copy-done.4
  102.4 1.7 middle.1
  104.2 10.4 %backward_product.1 = bf16[16,256,512]{2,1,0:T(8,128)(2,1)S(1)} custom-call(s32[1]{0:T(128)} %bitcast.9.own_section, bf16[256,1024]{1,0:T(8,128)(2,1)S(1)} %get-tuple-element.12.back_ref, bf16[1024,8192]{1,0:T(8,128)(2,1)} %densify.1.dense_ref), custom_call_target="tpu_custom_call" | custom-call | flops 4294967296 | bytes 21495808 | tf_op jit(solution)/shard_map/backward_product/pallas_call | solution.py:162
  114.6 0.0 copy-start
  114.6 1.9 copy-done
  116.6 0.0 reduce-scatter.2.cloned.1.call-update
  116.6 0.0 all-reduce.2.cloned.1.call-start
  116.7 0.7 collective-permute-start.2
  117.3 0.0 all-reduce.2.cloned.1.call-update
  117.3 0.0 collective-permute-done.2
  117.4 70.2 %reduce-scatter.2.cloned.1.call-done = bf16[1,256,512]{2,1,0:T(8,128)(2,1)} async-done(((bf16[16,256,512]{2,1,0:T(8,128)(2,1)}), bf16[1,256,512]{2,1,0:T(8,128)(2,1)}) %reduce-scatter.2.cloned.1.call-update) | async-done | bytes 262160 | tf_op jit(solution)/shard_map/reduce_scatter | solution.py:224
  187.6 1.0 fusion.1
  188.6 0.8 copy.13
  189.4 129.2 %all-reduce.2.cloned.1.call-done = f32[256,256]{1,0:T(8,128)} async-done(((f32[256,256]{1,0:T(8,128)}), f32[256,256]{1,0:T(8,128)}) %all-reduce.2.cloned.1.call-update) | async-done | bytes 262160 | tf_op jit(solution)/shard_map/psum | solution.py:222
  318.6 1.7 copy.15
  (1 shorter events, 0.0 us)
Async XLA Ops:
  7.2 66.9 %all-gather.2.cloned.1.call-start = ((), (), s32[]{:S(2)}) async-start(), calls=%async_computation.1 | async-start | bytes 4456448 | tf_op jit(solution)/shard_map/all_gather | solution.py:211
  9.1 0.7 collective-permute-start
  9.8 0.7 copy-start.7
  10.5 177.1 %reduce-scatter.2.cloned.1.call-start = ((), (), s32[]{:S(2)}) async-start(), calls=%async_computation.3 | async-start | bytes 4456448 | tf_op jit(solution)/shard_map/reduce_scatter | solution.py:224
  12.0 0.7 copy-start.5
  12.7 0.7 copy-start.6
  74.1 2.2 copy-start.1
  76.3 13.3 %copy-start.8 = (bf16[1024]{0:T(1024)(128)(2,1)S(1)}, bf16[1024]{0:T(1024)(128)(2,1)}, u32[]{:S(2)}) copy-start(bf16[1024]{0:T(1024)(128)(2,1)} %param.9) | copy-start | bytes 6148
  76.3 26.1 %copy-start.2 = (bf16[1024,256]{1,0:T(8,128)(2,1)S(1)}, bf16[1024,256]{1,0:T(8,128)(2,1)}, u32[]{:S(2)}) copy-start(bf16[1024,256]{1,0:T(8,128)(2,1)} %feats_ref.1) | copy-start | bytes 1572868
  76.3 26.1 %copy-start.3 = (bf16[1024,256]{1,0:T(8,128)(2,1)S(1)}, bf16[1024,256]{1,0:T(8,128)(2,1)}, u32[]{:S(2)}) copy-start(bf16[1024,256]{1,0:T(8,128)(2,1)} %cot_ref.1) | copy-start | bytes 1572868
  76.3 26.1 %copy-start.4 = (bf16[256,256]{1,0:T(8,128)(2,1)S(1)}, bf16[256,256]{1,0:T(8,128)(2,1)}, u32[]{:S(2)}) copy-start(bf16[256,256]{1,0:T(8,128)(2,1)} %weight_ref.1) | copy-start | bytes 393220
  88.1 14.3 %collective-permute-start.1 = (bf16[1024,256]{1,0:T(8,128)(2,1)}, bf16[1024,256]{1,0:T(8,128)(2,1)S(1)}, u32[]{:S(2)}, u32[]{:S(2)}) collective-permute-start(bf16[1024,256]{1,0:T(8,128)(2,1)} %get-tuple-element.9), channel_id=1, source_target_pairs={{0,1},{1,0},{2,3},{3,2},{4,5},{5,4},{6,7},{7,6},{8,9},{9,8},{10,11... | collective-permute-start | bytes 1572872 | tf_op jit(solution)/shard_map/ppermute | solution.py:216
  114.6 1.9 copy-start
  116.6 202.0 %all-reduce.2.cloned.1.call-start = ((), (), s32[]{:S(2)}) async-start(), calls=%async_computation.2 | async-start | bytes 524288 | tf_op jit(solution)/shard_map/psum | solution.py:222
  116.7 0.7 collective-permute-start.2
Sparse Core Ops, SparseCore 0:
  10.7 63.3 all-gather.1
  116.7 70.8 reduce-scatter.1
  194.6 123.9 all-reduce.1

commit v2 on v1

--- a/solution.py
+++ b/solution.py
@@ -179,6 +179,15 @@
         ),
         name="backward_product",
     )(own_section.reshape(1), back, dense)
+
+
+def sum_over_all(value, sizes):
+    for axis, size in sizes:
+        step = 1
+        while step < size:
+            value = value + lax.ppermute(value, axis, [(at, at ^ step) for at in range(size)])
+            step *= 2
+    return value
 
 
 def shards(features, inv_sqrt_degree, weight, tile_vals, tile_row, tile_col, tile_count, cotangent):
@@ -219,7 +228,7 @@
     activated, local_grad, back = middle(
         replica, own, other, features, degree, weight, cotangent, share, grad_factor
     )
-    weight_grad = lax.psum(local_grad, ("rows", "rep"))
+    weight_grad = sum_over_all(local_grad, (("rep", rep_count), ("rows", rows_count)))
     terms = backward(block_row - replica * sections, back, dense, sections, rep_count)
     gathered = lax.psum_scatter(terms, "rows", scatter_dimension=0, tiled=False)
     feature_grad = (placed_degree[:, None] * gathered.astype(jnp.float32).T).astype(jnp.bfloat16)

time: 327 us -> 201 us (0.61)
  waiting for transfers between devices: 262 us -> 130 us
  starting transfers between devices: 2.93 us -> 8.61 us
    psum x1 -> x0, waiting for transfers between devices: 129 us -> none  [shards(): weight_grad = lax.psum(local_grad, ('rows', 'rep'))]
    reduce_scatter x1, waiting for transfers between devices: 70.2 us -> 23 us  [shards(): gathered = lax.psum_scatter(terms, 'rows', scatter_dimension=0, tiled=False)]
    ppermute x0 -> x5, waiting for transfers between devices: none -> 44.8 us  [sum_over_all(): lax.ppermute(value, axis, [(at, at ^ step) for at in range(size)])]
    ppermute x0 -> x5, starting transfers between devices: none -> 5.73 us  [sum_over_all(): lax.ppermute(value, axis, [(at, at ^ step) for at in range(size)])]
    unnamed x20 -> x19, local copies, waits for them, and re-layouts: 8.71 us -> 7.04 us
  transfers between devices with their start and end apart: 6 -> 10, of which waited for: 4 -> 8; matrix products, arithmetic and copies ran while one was open for 1% -> 1% of each run, Pallas kernels for 3% -> 5%
where the time goes in v2:
time: 201 us; the launch traced here: 200 us
  waiting for transfers between devices  130 us (65%)
  Pallas kernels  34.7 us (17%)
  between operations  14.2 us (7%)
  starting transfers between devices  8.61 us (4%)
  local copies, waits for them, and re-layouts  8.03 us (4%)
  other arithmetic  4.44 us (2%)
    all_gather x1, waiting for transfers between devices, shards(): source = lax.all_gather(placed, 'rows', axis=0, tiled=True)  49.9 us
    ppermute x5, waiting for transfers between devices, sum_over_all(): lax.ppermute(value, axis, [(at, at ^ step) for at in range(size)])  44.8 us
    reduce_scatter x1, waiting for transfers between devices, shards(): gathered = lax.psum_scatter(terms, 'rows', scatter_dimension=0, tiled=False)  23 us
    ppermute x1, waiting for transfers between devices, shards(): other = lax.ppermute(sent, 'rep', [(0, 1), (1, 0)])  12.6 us
    pallas_call x1, Pallas kernels, forward(): pl.pallas_call(forward_kernel, out_shape=(jax.ShapeDtypeStruct((block, wi...  11.8 us
    pallas_call x1, Pallas kernels, densify(): pl.pallas_call(functools.partial(densify_kernel, per_block), out_shape=ja...  10.8 us
    pallas_call x1, Pallas kernels, backward(): pl.pallas_call(backward_kernel, out_shape=jax.ShapeDtypeStruct((sections...  10.4 us
    unnamed x19, local copies, waits for them, and re-layouts  7.04 us
  transfers between devices with their start and end apart: 10, of which 8 were waited for; matrix products, arithmetic and copies ran while one was open for 1% of the time, Pallas kernels for 5%

profile of v2, /device:TPU:0, one launch (start us, length us, event | category | flops | bytes accessed | tf_op | source)
XLA Modules:
  0.0 200.2 jit_solution(11312316350740113567)
XLA Ops:
  7.2 0.0 all-gather.2.cloned.1.call-start
  7.2 0.8 dynamic_slice.6
  8.0 1.1 multiply_convert_fusion
  9.1 0.7 collective-permute-start
  9.7 0.0 collective-permute-done
  9.8 0.0 copy-start.7
  9.8 0.7 copy-done.7
  10.5 0.0 all-gather.2.cloned.1.call-update
  10.5 0.0 reduce-scatter.2.cloned.1.call-start
  10.5 0.8 reduce-window.9
  11.4 0.7 bitcast_subtract_fusion.starts
  12.0 0.0 copy-start.5
  12.0 0.7 copy-done.5
  12.7 0.0 copy-start.6
  12.7 0.7 copy-done.6
  13.4 10.8 %densify.1.dense_ref = bf16[1024,8192]{1,0:T(8,128)(2,1)} custom-call(s32[8]{0:T(128)S(1)} %bitcast_subtract_fusion.starts, s32[8]{0:T(128)S(1)} %bitcast.21, s32[256]{0:T(256)S(1)} %bitcast.19, s32[256]{0:T(256)S(1)} %bitcast.20, bf16[256,128,128]{2,1,0:T(8,128)(2,1)} %bitcast.22), custom_call_target="tpu_custom_call" | custom-call | bytes 25165824 | tf_op jit(solution)/shard_map/densify/pallas_call | solution.py:30
  24.2 49.9 %all-gather.2.cloned.1.call-done.source_ref = bf16[8192,256]{1,0:T(8,128)(2,1)} async-done(((bf16[512,256]{1,0:T(8,128)(2,1)}), bf16[8192,256]{1,0:T(8,128)(2,1)}) %all-gather.2.cloned.1.call-update) | async-done | bytes 4194320 | tf_op jit(solution)/shard_map/all_gather | solution.py:220
  74.1 0.0 copy-start.1
  74.1 2.2 %copy-done.1 = bf16[8192,256]{1,0:T(8,128)(2,1)S(1)} copy-done((bf16[8192,256]{1,0:T(8,128)(2,1)S(1)}, bf16[8192,256]{1,0:T(8,128)(2,1)}, u32[]{:S(2)}) %copy-start.1) | copy-done | bytes 4194328
  76.3 0.0 copy-start.8
  76.3 0.0 copy-start.2
  76.3 0.0 copy-start.3
  76.3 0.0 copy-start.4
  76.3 11.8 %forward_product.1 = (f32[1024,256]{1,0:T(8,128)S(1)}, bf16[1024,256]{1,0:T(8,128)(2,1)}) custom-call(bf16[1024,8192]{1,0:T(8,128)(2,1)} %densify.1.dense_ref, bf16[8192,256]{1,0:T(8,128)(2,1)S(1)} %copy-done.1), custom_call_target="tpu_custom_call" | custom-call | flops 4294967296 | bytes 22544384 | tf_op jit(solution)/shard_map/forward_product/pallas_call | solution.py:68
  88.1 1.5 collective-permute-start.1
  89.6 0.0 copy-done.8
  89.6 0.2 copy.12.deg_col_ref
  89.9 12.6 %collective-permute-done.1.other_ref = bf16[1024,256]{1,0:T(8,128)(2,1)S(1)} collective-permute-done((bf16[1024,256]{1,0:T(8,128)(2,1)}, bf16[1024,256]{1,0:T(8,128)(2,1)S(1)}, u32[]{:S(2)}, u32[]{:S(2)}) %collective-permute-start.1) | collective-permute-done | bytes 524320 | tf_op jit(solution)/shard_map/ppermute | solution.py:225
  102.4 0.0 copy-done.2
  102.4 0.0 copy-done.3
  102.4 0.0 copy-done.4
  102.4 1.6 middle.1
  104.1 10.4 %backward_product.1 = bf16[16,256,512]{2,1,0:T(8,128)(2,1)S(1)} custom-call(s32[1]{0:T(128)} %bitcast.9.own_section, bf16[256,1024]{1,0:T(8,128)(2,1)S(1)} %get-tuple-element.12.back_ref, bf16[1024,8192]{1,0:T(8,128)(2,1)} %densify.1.dense_ref), custom_call_target="tpu_custom_call" | custom-call | flops 4294967296 | bytes 21495808 | tf_op jit(solution)/shard_map/backward_product/pallas_call | solution.py:162
  114.5 0.0 copy-start
  114.5 1.9 copy-done
  116.5 0.0 reduce-scatter.2.cloned.1.call-update
  116.5 1.5 collective-permute-start.2
  118.0 6.2 %collective-permute-done.2 = f32[256,256]{1,0:T(8,128)S(1)} collective-permute-done((f32[256,256]{1,0:T(8,128)S(1)}, f32[256,256]{1,0:T(8,128)S(1)}, u32[]{:S(2)}, u32[]{:S(2)}) %collective-permute-start.2) | collective-permute-done | bytes 262176 | tf_op jit(solution)/shard_map/ppermute | solution.py:188
  124.3 0.1 collective-permute-start.3
  124.3 1.5 collective-permute-done.3
  125.9 0.6 collective-permute-start.4
  126.5 7.8 %collective-permute-done.4 = f32[256,256]{1,0:T(8,128)S(1)} collective-permute-done((f32[256,256]{1,0:T(8,128)S(1)}, f32[256,256]{1,0:T(8,128)S(1)}, u32[]{:S(2)}, u32[]{:S(2)}) %collective-permute-start.4) | collective-permute-done | bytes 262176 | tf_op jit(solution)/shard_map/ppermute | solution.py:188
  134.3 1.6 collective-permute-start.5
  135.9 6.0 %collective-permute-done.5 = f32[256,256]{1,0:T(8,128)S(1)} collective-permute-done((f32[256,256]{1,0:T(8,128)S(1)}, f32[256,256]{1,0:T(8,128)S(1)}, u32[]{:S(2)}, u32[]{:S(2)}) %collective-permute-start.5) | collective-permute-done | bytes 262176 | tf_op jit(solution)/shard_map/ppermute | solution.py:188
  142.0 1.9 collective-permute-start.6
  143.9 0.6 collective-permute-start.7
  144.6 23.2 %collective-permute-done.6 = f32[256,256]{1,0:T(8,128)S(1)} collective-permute-done((f32[256,256]{1,0:T(8,128)S(1)}, f32[256,256]{1,0:T(8,128)S(1)}, u32[]{:S(2)}, u32[]{:S(2)}) %collective-permute-start.6) | collective-permute-done | bytes 262176 | tf_op jit(solution)/shard_map/ppermute | solution.py:188
  167.8 0.7 add.26
  168.5 0.0 collective-permute-done.7
  168.5 23.0 %reduce-scatter.2.cloned.1.call-done = bf16[1,256,512]{2,1,0:T(8,128)(2,1)} async-done(((bf16[16,256,512]{2,1,0:T(8,128)(2,1)}), bf16[1,256,512]{2,1,0:T(8,128)(2,1)}) %reduce-scatter.2.cloned.1.call-update) | async-done | bytes 262160 | tf_op jit(solution)/shard_map/reduce_scatter | solution.py:233
  191.6 1.0 fusion.1
  192.6 0.8 copy.13
  (5 shorter events, 0.1 us)
Async XLA Ops:
  7.2 66.9 %all-gather.2.cloned.1.call-start = ((), (), s32[]{:S(2)}) async-start(), calls=%async_computation.1 | async-start | bytes 4456448 | tf_op jit(solution)/shard_map/all_gather | solution.py:220
  9.1 0.7 collective-permute-start
  9.8 0.7 copy-start.7
  10.5 181.1 %reduce-scatter.2.cloned.1.call-start = ((), (), s32[]{:S(2)}) async-start(), calls=%async_computation.2 | async-start | bytes 4456448 | tf_op jit(solution)/shard_map/reduce_scatter | solution.py:233
  12.0 0.7 copy-start.5
  12.7 0.7 copy-start.6
  74.1 2.2 %copy-start.1 = (bf16[8192,256]{1,0:T(8,128)(2,1)S(1)}, bf16[8192,256]{1,0:T(8,128)(2,1)}, u32[]{:S(2)}) copy-start(bf16[8192,256]{1,0:T(8,128)(2,1)} %all-gather.2.cloned.1.call-done.source_ref) | copy-start | bytes 12582916
  76.3 13.3 %copy-start.8 = (bf16[1024]{0:T(1024)(128)(2,1)S(1)}, bf16[1024]{0:T(1024)(128)(2,1)}, u32[]{:S(2)}) copy-start(bf16[1024]{0:T(1024)(128)(2,1)} %param.9) | copy-start | bytes 6148
  76.3 26.1 %copy-start.2 = (bf16[1024,256]{1,0:T(8,128)(2,1)S(1)}, bf16[1024,256]{1,0:T(8,128)(2,1)}, u32[]{:S(2)}) copy-start(bf16[1024,256]{1,0:T(8,128)(2,1)} %feats_ref.1) | copy-start | bytes 1572868
  76.3 26.1 %copy-start.3 = (bf16[1024,256]{1,0:T(8,128)(2,1)S(1)}, bf16[1024,256]{1,0:T(8,128)(2,1)}, u32[]{:S(2)}) copy-start(bf16[1024,256]{1,0:T(8,128)(2,1)} %cot_ref.1) | copy-start | bytes 1572868
  76.3 26.1 %copy-start.4 = (bf16[256,256]{1,0:T(8,128)(2,1)S(1)}, bf16[256,256]{1,0:T(8,128)(2,1)}, u32[]{:S(2)}) copy-start(bf16[256,256]{1,0:T(8,128)(2,1)} %weight_ref.1) | copy-start | bytes 393220
  88.1 14.3 %collective-permute-start.1 = (bf16[1024,256]{1,0:T(8,128)(2,1)}, bf16[1024,256]{1,0:T(8,128)(2,1)S(1)}, u32[]{:S(2)}, u32[]{:S(2)}) collective-permute-start(bf16[1024,256]{1,0:T(8,128)(2,1)} %get-tuple-element.9), channel_id=1, source_target_pairs={{0,1},{1,0},{2,3},{3,2},{4,5},{5,4},{6,7},{7,6},{8,9},{9,8},{10,11... | collective-permute-start | bytes 1572872 | tf_op jit(solution)/shard_map/ppermute | solution.py:225
  114.5 2.0 copy-start
  116.5 7.7 %collective-permute-start.2 = (f32[256,256]{1,0:T(8,128)S(1)}, f32[256,256]{1,0:T(8,128)S(1)}, u32[]{:S(2)}, u32[]{:S(2)}) collective-permute-start(f32[256,256]{1,0:T(8,128)S(1)} %get-tuple-element.11), channel_id=1, source_target_pairs={{0,1},{1,0},{2,3},{3,2},{4,5},{5,4},{6,7},{7,6},{8,9},{9,8},{10,11... | collective-permute-start | bytes 786440 | tf_op jit(solution)/shard_map/ppermute | solution.py:188
  124.3 1.6 collective-permute-start.3
  125.9 8.4 %collective-permute-start.4 = (f32[256,256]{1,0:T(8,128)S(1)}, f32[256,256]{1,0:T(8,128)S(1)}, u32[]{:S(2)}, u32[]{:S(2)}) collective-permute-start(f32[256,256]{1,0:T(8,128)S(1)} %add.23), channel_id=1, source_target_pairs={{0,4},{2,6},{4,0},{6,2},{8,12},{10,14},{12,8},{14,10},{16,20},{18,... | collective-permute-start | bytes 786440 | tf_op jit(solution)/shard_map/ppermute | solution.py:188
  134.3 7.6 %collective-permute-start.5 = (f32[256,256]{1,0:T(8,128)S(1)}, f32[256,256]{1,0:T(8,128)S(1)}, u32[]{:S(2)}, u32[]{:S(2)}) collective-permute-start(f32[256,256]{1,0:T(8,128)S(1)} %add.24), channel_id=1, source_target_pairs={{0,8},{2,10},{4,12},{6,14},{8,0},{10,2},{12,4},{14,6},{16,24},{18,... | collective-permute-start | bytes 786440 | tf_op jit(solution)/shard_map/ppermute | solution.py:188
  142.0 25.8 %collective-permute-start.6 = (f32[256,256]{1,0:T(8,128)S(1)}, f32[256,256]{1,0:T(8,128)S(1)}, u32[]{:S(2)}, u32[]{:S(2)}) collective-permute-start(f32[256,256]{1,0:T(8,128)S(1)} %add.25), channel_id=1, source_target_pairs={{0,16},{2,18},{4,20},{6,22},{8,24},{10,26},{12,28},{14,30},{16,0},... | collective-permute-start | bytes 786440 | tf_op jit(solution)/shard_map/ppermute | solution.py:188
  143.9 24.6 %collective-permute-start.7 = (f32[512]{0:T(512)S(1)}, f32[512]{0:T(512)S(1)}, u32[]{:S(2)}, u32[]{:S(2)}) collective-permute-start(f32[512]{0:T(512)S(1)} %dynamic_slice.6), channel_id=1, source_target_pairs={{0,0},{1,2},{2,4},{3,6},{4,8},{5,10},{6,12},{7,14},{8,16},{9,18},{... | collective-permute-start | bytes 6152 | tf_op jit(solution)/shard_map/ppermute | solution.py:219
Sparse Core Ops, SparseCore 0:
  10.7 63.3 all-gather.1
  116.6 74.8 reduce-scatter.1

commit v3 on v2

--- a/solution.py
+++ b/solution.py
@@ -61,8 +61,8 @@
         sent_ref[...] = total_ref[...].astype(sent_ref.dtype)
 
 
-def forward(dense, source, sections):
-    block, depth = dense.shape
+def forward(dense, source, sections, half):
+    block, depth = dense.shape[0] // 2, dense.shape[1]
     width = source.shape[-1]
     step = depth // sections
     return pl.pallas_call(
@@ -73,7 +73,7 @@
         ),
         grid=(sections,),
         in_specs=[
-            pl.BlockSpec((block, step), lambda s: (0, s)),
+            pl.BlockSpec((block, step), lambda s: (half, s)),
             pl.BlockSpec((step, width), lambda s: (s, 0)),
         ],
         out_specs=(
@@ -86,17 +86,23 @@
             bytes_accessed=2 * (block * depth + depth * width) + 6 * block * width,
             transcendentals=0,
         ),
-        name="forward_product",
+        name="forward_product_" + str(half),
     )(dense, source)
 
 
 def middle_kernel(
-    share, factor, replica, own_ref, other_ref, feats_ref, deg_col_ref, deg_row_ref, weight_ref,
+    share, factor, replica, own0_ref, own1_ref, other0_ref, other1_ref, feats_ref, deg_col_ref, deg_row_ref, weight_ref,
     cot_ref, act_ref, grad_ref, back_ref, prop_ref, pre_ref, full_ref,
 ):
     degree = deg_col_ref[...]
     scaled = (degree * feats_ref[...].astype(jnp.float32)).astype(jnp.bfloat16)
-    summed = own_ref[...] + other_ref[...].astype(jnp.float32)
+    summed = jnp.concatenate(
+        [
+            own0_ref[...] + other0_ref[...].astype(jnp.float32),
+            own1_ref[...] + other1_ref[...].astype(jnp.float32),
+        ],
+        axis=0,
+    )
     propagated = (degree * (summed + scaled.astype(jnp.float32))).astype(jnp.bfloat16)
     weight = weight_ref[...]
     preact = jnp.dot(propagated, weight, preferred_element_type=jnp.float32)
@@ -129,7 +135,7 @@
             jax.ShapeDtypeStruct((width, width), jnp.float32),
             jax.ShapeDtypeStruct((width, block), jnp.bfloat16),
         ),
-        in_specs=[pl.BlockSpec(memory_space=pltpu.SMEM)] + [vmem] * 7,
+        in_specs=[pl.BlockSpec(memory_space=pltpu.SMEM)] + [vmem] * 9,
         out_specs=(vmem, vmem, vmem),
         scratch_shapes=[pltpu.VMEM((block, width), jnp.bfloat16)] * 3,
         compiler_params=pltpu.CompilerParams(vmem_limit_bytes=LIMIT),
@@ -138,7 +144,7 @@
         ),
         name="middle",
     )(
-        replica.reshape(1), own, other, features, degree.reshape(block, 1), degree.reshape(1, block),
+        replica.reshape(1), *own, *other, features, degree.reshape(block, 1), degree.reshape(1, block),
         weight, cotangent,
     )
 
@@ -220,11 +226,14 @@
     source = lax.all_gather(placed, "rows", axis=0, tiled=True)
 
     dense = densify(tile_vals[0], tile_row[0], tile_col[0], starts, ends, per_block, sections)
-    own, sent = forward(dense, source, sections)
-    if rep_count == 2:
-        other = lax.ppermute(sent, "rep", [(0, 1), (1, 0)])
-    else:
-        other = lax.psum(own, "rep") - own
+    own, other = [], []
+    for half in range(2):
+        part, sent = forward(dense, source, sections, half)
+        own.append(part)
+        if rep_count == 2:
+            other.append(lax.ppermute(sent, "rep", [(0, 1), (1, 0)]))
+        else:
+            other.append(lax.psum(part, "rep") - part)
     activated, local_grad, back = middle(
         replica, own, other, features, degree, weight, cotangent, share, grad_factor
     )

time: 201 us -> 199 us (0.990)
  waiting for transfers between devices: 130 us -> 124 us
  Pallas kernels: 34.7 us -> 39.7 us
    ppermute x1 -> x2, waiting for transfers between devices: 12.6 us -> 7.58 us  [shards(): other.append(lax.ppermute(sent, 'rep', [(0, 1), (1, 0)]))]
    pallas_call x1 -> x2, Pallas kernels: 11.8 us -> 16 us  [forward(): pl.pallas_call(forward_kernel, out_shape=(jax.ShapeDtypeStruct((block, wi...]
  transfers between devices with their start and end apart: 10 -> 11, of which waited for: 8 -> 8; matrix products, arithmetic and copies ran while one was open for 1% -> 1% of each run, Pallas kernels for 5% -> 10%
where the time goes in v3:
time: 199 us
  waiting for transfers between devices  124 us (62%)
  Pallas kernels  39.7 us (20%)
  between operations  14.2 us (7%)
  starting transfers between devices  8.09 us (4%)
  local copies, waits for them, and re-layouts  8.03 us (4%)
  other arithmetic  4.44 us (2%)
    all_gather x1, waiting for transfers between devices, shards(): source = lax.all_gather(placed, 'rows', axis=0, tiled=True)  49.1 us
    ppermute x5, waiting for transfers between devices, sum_over_all(): lax.ppermute(value, axis, [(at, at ^ step) for at in range(size)])  45.6 us
    reduce_scatter x1, waiting for transfers between devices, shards(): gathered = lax.psum_scatter(terms, 'rows', scatter_dimension=0, tiled=False)  21.8 us
    pallas_call x2, Pallas kernels, forward(): pl.pallas_call(forward_kernel, out_shape=(jax.ShapeDtypeStruct((block, wi...  16 us
    pallas_call x1, Pallas kernels, densify(): pl.pallas_call(functools.partial(densify_kernel, per_block), out_shape=ja...  11.7 us
    pallas_call x1, Pallas kernels, backward(): pl.pallas_call(backward_kernel, out_shape=jax.ShapeDtypeStruct((sections...  10.4 us
    ppermute x2, waiting for transfers between devices, shards(): other.append(lax.ppermute(sent, 'rep', [(0, 1), (1, 0)]))  7.58 us
    unnamed x19, local copies, waits for them, and re-layouts  7.04 us
  transfers between devices with their start and end apart: 11, of which 8 were waited for; matrix products, arithmetic and copies ran while one was open for 1% of the time, Pallas kernels for 10%

profile of v3, /device:TPU:0, one launch (start us, length us, event | category | flops | bytes accessed | tf_op | source)
XLA Modules:
  0.0 198.6 jit_solution(427241684311598460)
XLA Ops:
  7.2 0.0 all-gather.2.cloned.1.call-start
  7.2 0.8 dynamic_slice.6
  8.0 1.1 multiply_convert_fusion
  9.1 0.7 collective-permute-start
  9.7 0.0 collective-permute-done
  9.8 0.0 copy-start.7
  9.8 0.7 copy-done.7
  10.5 0.0 all-gather.2.cloned.1.call-update
  10.5 0.0 reduce-scatter.2.cloned.1.call-start
  10.5 0.8 reduce-window.9
  11.4 0.7 bitcast_subtract_fusion.starts
  12.0 0.0 copy-start.5
  12.0 0.7 copy-done.5
  12.7 0.0 copy-start.6
  12.7 0.7 copy-done.6
  13.4 11.7 %densify.1.dense_ref = bf16[1024,8192]{1,0:T(8,128)(2,1)} custom-call(s32[8]{0:T(128)S(1)} %bitcast_subtract_fusion.starts, s32[8]{0:T(128)S(1)} %bitcast.21, s32[256]{0:T(256)S(1)} %bitcast.19, s32[256]{0:T(256)S(1)} %bitcast.20, bf16[256,128,128]{2,1,0:T(8,128)(2,1)} %bitcast.22), custom_call_target="tpu_custom_call" | custom-call | bytes 25165824 | tf_op jit(solution)/shard_map/densify/pallas_call | solution.py:30
  25.0 49.1 %all-gather.2.cloned.1.call-done.source_ref = bf16[8192,256]{1,0:T(8,128)(2,1)} async-done(((bf16[512,256]{1,0:T(8,128)(2,1)}), bf16[8192,256]{1,0:T(8,128)(2,1)}) %all-gather.2.cloned.1.call-update) | async-done | bytes 4194320 | tf_op jit(solution)/shard_map/all_gather | solution.py:226
  74.1 0.0 copy-start
  74.1 2.2 %copy-done = bf16[8192,256]{1,0:T(8,128)(2,1)S(1)} copy-done((bf16[8192,256]{1,0:T(8,128)(2,1)S(1)}, bf16[8192,256]{1,0:T(8,128)(2,1)}, u32[]{:S(2)}) %copy-start) | copy-done | bytes 4194328
  76.3 7.6 %forward_product_1.1 = (f32[512,256]{1,0:T(8,128)S(1)}, bf16[512,256]{1,0:T(8,128)(2,1)S(1)}) custom-call(bf16[1024,8192]{1,0:T(8,128)(2,1)} %densify.1.dense_ref, bf16[8192,256]{1,0:T(8,128)(2,1)S(1)} %copy-done), custom_call_target="tpu_custom_call" | custom-call | flops 2147483648 | bytes 13369344 | tf_op jit(solution)/shard_map/forward_product_1/pallas_call | solution.py:68
  83.9 0.0 copy-start.8
  83.9 0.0 copy-start.2
  84.0 0.0 copy-start.3
  84.0 0.0 copy-start.4
  84.0 1.5 collective-permute-start.2
  85.5 8.3 %forward_product_0.1 = (f32[512,256]{1,0:T(8,128)S(1)}, bf16[512,256]{1,0:T(8,128)(2,1)}) custom-call(bf16[1024,8192]{1,0:T(8,128)(2,1)} %densify.1.dense_ref, bf16[8192,256]{1,0:T(8,128)(2,1)S(1)} %copy-done), custom_call_target="tpu_custom_call" | custom-call | flops 2147483648 | bytes 13369344 | tf_op jit(solution)/shard_map/forward_product_0/pallas_call | solution.py:68
  93.8 0.6 collective-permute-start.1
  94.4 0.0 copy-done.8
  94.4 0.2 copy.12.deg_col_ref
  94.6 0.0 collective-permute-done.2.other1_ref
  94.7 7.6 %collective-permute-done.1.other0_ref = bf16[512,256]{1,0:T(8,128)(2,1)S(1)} collective-permute-done((bf16[512,256]{1,0:T(8,128)(2,1)}, bf16[512,256]{1,0:T(8,128)(2,1)S(1)}, u32[]{:S(2)}, u32[]{:S(2)}) %collective-permute-start.1) | collective-permute-done | bytes 262176 | tf_op jit(solution)/shard_map/ppermute | solution.py:234
  102.2 0.0 copy-done.2
  102.2 0.0 copy-done.3
  102.2 0.0 copy-done.4
  102.2 1.6 middle.1
  103.9 10.4 %backward_product.1 = bf16[16,256,512]{2,1,0:T(8,128)(2,1)S(1)} custom-call(s32[1]{0:T(128)} %bitcast.9.own_section, bf16[256,1024]{1,0:T(8,128)(2,1)S(1)} %get-tuple-element.16.back_ref, bf16[1024,8192]{1,0:T(8,128)(2,1)} %densify.1.dense_ref), custom_call_target="tpu_custom_call" | custom-call | flops 4294967296 | bytes 21495808 | tf_op jit(solution)/shard_map/backward_product/pallas_call | solution.py:168
  114.3 0.0 copy-start.1
  114.3 1.9 copy-done.1
  116.3 0.0 reduce-scatter.2.cloned.1.call-update
  116.3 0.6 collective-permute-start.3
  116.9 6.8 %collective-permute-done.3 = f32[256,256]{1,0:T(8,128)S(1)} collective-permute-done((f32[256,256]{1,0:T(8,128)S(1)}, f32[256,256]{1,0:T(8,128)S(1)}, u32[]{:S(2)}, u32[]{:S(2)}) %collective-permute-start.3) | collective-permute-done | bytes 262176 | tf_op jit(solution)/shard_map/ppermute | solution.py:194
  123.7 0.1 collective-permute-start.4
  123.8 1.6 collective-permute-done.4
  125.4 0.6 collective-permute-start.5
  126.0 7.9 %collective-permute-done.5 = f32[256,256]{1,0:T(8,128)S(1)} collective-permute-done((f32[256,256]{1,0:T(8,128)S(1)}, f32[256,256]{1,0:T(8,128)S(1)}, u32[]{:S(2)}, u32[]{:S(2)}) %collective-permute-start.5) | collective-permute-done | bytes 262176 | tf_op jit(solution)/shard_map/ppermute | solution.py:194
  133.9 1.5 collective-permute-start.6
  135.4 6.1 %collective-permute-done.6 = f32[256,256]{1,0:T(8,128)S(1)} collective-permute-done((f32[256,256]{1,0:T(8,128)S(1)}, f32[256,256]{1,0:T(8,128)S(1)}, u32[]{:S(2)}, u32[]{:S(2)}) %collective-permute-start.6) | collective-permute-done | bytes 262176 | tf_op jit(solution)/shard_map/ppermute | solution.py:194
  141.5 1.8 collective-permute-start.7
  143.3 0.6 collective-permute-start.8
  144.0 23.4 %collective-permute-done.7 = f32[256,256]{1,0:T(8,128)S(1)} collective-permute-done((f32[256,256]{1,0:T(8,128)S(1)}, f32[256,256]{1,0:T(8,128)S(1)}, u32[]{:S(2)}, u32[]{:S(2)}) %collective-permute-start.7) | collective-permute-done | bytes 262176 | tf_op jit(solution)/shard_map/ppermute | solution.py:194
  167.3 0.7 add.26
  168.1 0.0 collective-permute-done.8
  168.1 21.8 %reduce-scatter.2.cloned.1.call-done = bf16[1,256,512]{2,1,0:T(8,128)(2,1)} async-done(((bf16[16,256,512]{2,1,0:T(8,128)(2,1)}), bf16[1,256,512]{2,1,0:T(8,128)(2,1)}) %reduce-scatter.2.cloned.1.call-update) | async-done | bytes 262160 | tf_op jit(solution)/shard_map/reduce_scatter | solution.py:242
  189.9 1.0 fusion.1
  190.9 0.8 copy.13
  (5 shorter events, 0.1 us)
Async XLA Ops:
  7.2 66.9 %all-gather.2.cloned.1.call-start = ((), (), s32[]{:S(2)}) async-start(), calls=%async_computation.1 | async-start | bytes 4456448 | tf_op jit(solution)/shard_map/all_gather | solution.py:226
  9.1 0.7 collective-permute-start
  9.8 0.7 copy-start.7
  10.5 179.4 %reduce-scatter.2.cloned.1.call-start = ((), (), s32[]{:S(2)}) async-start(), calls=%async_computation.2 | async-start | bytes 4456448 | tf_op jit(solution)/shard_map/reduce_scatter | solution.py:242
  12.0 0.7 copy-start.5
  12.7 0.7 copy-start.6
  74.1 2.2 %copy-start = (bf16[8192,256]{1,0:T(8,128)(2,1)S(1)}, bf16[8192,256]{1,0:T(8,128)(2,1)}, u32[]{:S(2)}) copy-start(bf16[8192,256]{1,0:T(8,128)(2,1)} %all-gather.2.cloned.1.call-done.source_ref) | copy-start | bytes 12582916
  83.9 10.5 %copy-start.8 = (bf16[1024]{0:T(1024)(128)(2,1)S(1)}, bf16[1024]{0:T(1024)(128)(2,1)}, u32[]{:S(2)}) copy-start(bf16[1024]{0:T(1024)(128)(2,1)} %param.9) | copy-start | bytes 6148
  83.9 18.3 %copy-start.2 = (bf16[1024,256]{1,0:T(8,128)(2,1)S(1)}, bf16[1024,256]{1,0:T(8,128)(2,1)}, u32[]{:S(2)}) copy-start(bf16[1024,256]{1,0:T(8,128)(2,1)} %feats_ref.1) | copy-start | bytes 1572868
  84.0 18.3 %copy-start.3 = (bf16[1024,256]{1,0:T(8,128)(2,1)S(1)}, bf16[1024,256]{1,0:T(8,128)(2,1)}, u32[]{:S(2)}) copy-start(bf16[1024,256]{1,0:T(8,128)(2,1)} %cot_ref.1) | copy-start | bytes 1572868
  84.0 18.3 %copy-start.4 = (bf16[256,256]{1,0:T(8,128)(2,1)S(1)}, bf16[256,256]{1,0:T(8,128)(2,1)}, u32[]{:S(2)}) copy-start(bf16[256,256]{1,0:T(8,128)(2,1)} %weight_ref.1) | copy-start | bytes 393220
  84.0 10.7 %collective-permute-start.2 = (bf16[512,256]{1,0:T(8,128)(2,1)S(1)}, bf16[512,256]{1,0:T(8,128)(2,1)S(1)}, u32[]{:S(2)}, u32[]{:S(2)}) collective-permute-start(bf16[512,256]{1,0:T(8,128)(2,1)S(1)} %get-tuple-element.13), channel_id=1, source_target_pairs={{0,1},{1,0},{2,3},{3,2},{4,5},{5,4},{6,7},{7,6},{8,9},{9,8},{10,11... | collective-permute-start | bytes 786440 | tf_op jit(solution)/shard_map/ppermute | solution.py:234
  93.8 8.4 %collective-permute-start.1 = (bf16[512,256]{1,0:T(8,128)(2,1)}, bf16[512,256]{1,0:T(8,128)(2,1)S(1)}, u32[]{:S(2)}, u32[]{:S(2)}) collective-permute-start(bf16[512,256]{1,0:T(8,128)(2,1)} %get-tuple-element.12), channel_id=1, source_target_pairs={{0,1},{1,0},{2,3},{3,2},{4,5},{5,4},{6,7},{7,6},{8,9},{9,8},{10,11... | collective-permute-start | bytes 786440 | tf_op jit(solution)/shard_map/ppermute | solution.py:234
  114.3 1.9 copy-start.1
  116.3 7.4 %collective-permute-start.3 = (f32[256,256]{1,0:T(8,128)S(1)}, f32[256,256]{1,0:T(8,128)S(1)}, u32[]{:S(2)}, u32[]{:S(2)}) collective-permute-start(f32[256,256]{1,0:T(8,128)S(1)} %get-tuple-element.15), channel_id=1, source_target_pairs={{0,1},{1,0},{2,3},{3,2},{4,5},{5,4},{6,7},{7,6},{8,9},{9,8},{10,11... | collective-permute-start | bytes 786440 | tf_op jit(solution)/shard_map/ppermute | solution.py:194
  123.7 1.6 collective-permute-start.4
  125.4 8.4 %collective-permute-start.5 = (f32[256,256]{1,0:T(8,128)S(1)}, f32[256,256]{1,0:T(8,128)S(1)}, u32[]{:S(2)}, u32[]{:S(2)}) collective-permute-start(f32[256,256]{1,0:T(8,128)S(1)} %add.23), channel_id=1, source_target_pairs={{0,4},{2,6},{4,0},{6,2},{8,12},{10,14},{12,8},{14,10},{16,20},{18,... | collective-permute-start | bytes 786440 | tf_op jit(solution)/shard_map/ppermute | solution.py:194
  133.9 7.6 %collective-permute-start.6 = (f32[256,256]{1,0:T(8,128)S(1)}, f32[256,256]{1,0:T(8,128)S(1)}, u32[]{:S(2)}, u32[]{:S(2)}) collective-permute-start(f32[256,256]{1,0:T(8,128)S(1)} %add.24), channel_id=1, source_target_pairs={{0,8},{2,10},{4,12},{6,14},{8,0},{10,2},{12,4},{14,6},{16,24},{18,... | collective-permute-start | bytes 786440 | tf_op jit(solution)/shard_map/ppermute | solution.py:194
  141.5 25.8 %collective-permute-start.7 = (f32[256,256]{1,0:T(8,128)S(1)}, f32[256,256]{1,0:T(8,128)S(1)}, u32[]{:S(2)}, u32[]{:S(2)}) collective-permute-start(f32[256,256]{1,0:T(8,128)S(1)} %add.25), channel_id=1, source_target_pairs={{0,16},{2,18},{4,20},{6,22},{8,24},{10,26},{12,28},{14,30},{16,0},... | collective-permute-start | bytes 786440 | tf_op jit(solution)/shard_map/ppermute | solution.py:194
  143.3 24.8 %collective-permute-start.8 = (f32[512]{0:T(512)S(1)}, f32[512]{0:T(512)S(1)}, u32[]{:S(2)}, u32[]{:S(2)}) collective-permute-start(f32[512]{0:T(512)S(1)} %dynamic_slice.6), channel_id=1, source_target_pairs={{0,0},{1,2},{2,4},{3,6},{4,8},{5,10},{6,12},{7,14},{8,16},{9,18},{... | collective-permute-start | bytes 6152 | tf_op jit(solution)/shard_map/ppermute | solution.py:225
Sparse Core Ops, SparseCore 0:
  10.7 63.3 all-gather.1
  116.4 73.4 reduce-scatter.1
